TPU v7x, 128 devices: a whole 4x4x4 slice. The times are simulated.
128 devices in a mesh: row: 8 (over z, core), col: 16 (over x, y).
Axes of the slice: x: 4, y: 4, z: 4, core: 2. Of those that a mesh axis runs over, the one named last changes fastest.
Arguments:
- amplitudes: float32 [4, 1024, 64, 1024], P(None, 'col', 'row'), may hold values from -6 to 6
- cycle_weights: float32 [4, 1024, 1024], P(None, 'col', 'row'), may hold values from -0.09375 to 0.09375
- residual_in: float32 [1024, 64, 1024], P('col', 'row'), may hold values from -6 to 6
Outputs:
- residual_out: float32 [1024, 64, 1024], P('col', 'row')
All inputs are finite; a program needn't handle non-finite values.
Results may differ from a plain program's by a relative error of at most 0.0001.
Values sent between devices are 32-bit elements; how exact they have to be, the bound alone decides.
A program may use at most 192 MiB of HBM per device.

v0:
```python
import jax
import jax.numpy as jnp
from jax import lax
from jax.sharding import PartitionSpec as P


def shards(amplitudes, cycle_weights, residual_in):
    row_weights = lax.all_gather(cycle_weights, "row", axis=2, tiled=True)
    full_weights = lax.all_gather(row_weights, "col", axis=1, tiled=True)
    cycle_sum = jnp.einsum(
        "jbia,jbc->aic",
        lax.all_to_all(amplitudes, "col", split_axis=3, concat_axis=1, tiled=True),
        full_weights,
        precision=lax.Precision.HIGHEST,
        preferred_element_type=jnp.float32,
    )
    return residual_in + cycle_sum


def solution(mesh):
    return jax.shard_map(
        shards,
        mesh=mesh,
        in_specs=(P(None, "col", "row", None), P(None, "col", "row"), P("col", "row", None)),
        out_specs=P("col", "row", None),
        check_vma=False,
    )
```

profile of v0, /device:TPU:1, one launch (start us, length us, event | category | flops | bytes accessed | tf_op | source)
XLA Modules:
  0.0 356.2 jit_solution(5050010192621561453)
XLA Ops:
  6.5 0.0 all-gather.3.cloned.1.call-start
  6.5 0.7 all-gather.3.cloned.1.call-update
  7.3 0.0 all-gather.5.cloned.1.call-start
  7.3 29.0 %all-gather.3.cloned.1.call-done = f32[4,64,1024]{2,1,0:T(8,128)} async-done(((f32[4,64,128]{2,1,0:T(8,128)}), f32[4,64,1024]{2,1,0:T(8,128)}) %all-gather.3.cloned.1.call-update) | async-done | bytes 1048592 | tf_op jit(solution)/shard_map/all_gather | solution.py:8
  36.3 0.0 all-gather.5.cloned.1.call-update
  36.3 16.8 %copy.11 = f32[4,64,8,1024]{1,2,0,3:T(8,128)} copy(f32[4,64,8,1024]{3,2,1,0:T(8,128)} %param.3) | data formatting | bytes 16777216 | tf_op args[0]
  53.0 18.5 %reshape.2 = f32[16,1,131072]{2,1,0:T(1,128)} reshape(f32[1024,4,8,64]{3,2,1,0:T(8,128)} %bitcast.22) | data formatting | bytes 16777216
  71.6 168.3 %all_to_all.18 = f32[16,1,131072]{2,1,0:T(1,128)} all-to-all(f32[16,1,131072]{2,1,0:T(1,128)} %reshape.2), channel_id=1, replica_groups=mesh['row'=8,'col'=16] {'col'}, dimensions={0} | all-to-all | bytes 16777216 | tf_op jit(solution)/shard_map/all_to_all | solution.py:12
  239.9 0.5 broadcast
  240.4 25.1 %reduce = f32[16,131072]{1,0:T(8,128)} reduce(f32[16,1,131072]{2,1,0:T(1,128)} %all_to_all.18, f32[]{:T(128)} %broadcast), dimensions={1}, to_apply=%all_to_all.13.reduce_sub_computation | reduce | bytes 16777220 | tf_op jit(solution)/shard_map/all_to_all | solution.py:12
  265.5 17.3 %reshape.3 = f32[1024,4,8,64]{3,2,1,0:T(8,128)} reshape(f32[16,131072]{1,0:T(8,128)} %reduce) | data formatting | bytes 16777216
  282.9 17.7 %copy.18 = f32[4,64,8,16,64]{1,3,4,0,2:T(8,128)} copy(f32[4,64,8,16,64]{1,2,0,4,3:T(8,128)} %bitcast.23) | data formatting | bytes 16777216 | tf_op jit(solution)/shard_map/all_to_all | solution.py:12
  300.5 0.0 copy-start
  300.5 14.7 %all_to_all.16 = f32[4,1024,8,64]{1,3,0,2:T(8,128)} reshape(f32[4,16,64,8,64]{2,1,4,0,3:T(8,128)} %bitcast.24) | data formatting | bytes 16777216 | tf_op jit(solution)/shard_map/all_to_all | solution.py:12
  315.2 0.0 all-gather.5.cloned.1.call-done
  315.2 0.0 copy-done
  315.2 31.7 %bitcast_add_fusion = f32[64,8,1024]{2,0,1:T(8,128)S(1)} fusion(f32[64,8,1024]{2,1,0:T(8,128)S(1)} %copy-done, f32[4,1024,8,64]{1,3,0,2:T(8,128)} %all_to_all.16, f32[4,1024,1024]{2,1,0:T(8,128)} %all-gather.5.cloned.1.call-done), kind=kOutput, calls=%fused_computation.3 | convolution fusion | flops 25770328064 | bytes 29360128 | tf_op jit(solution)/shard_map/jbia,jbc->aic/dot_general | solution.py:10
  346.9 2.5 copy.14
Async XLA Ops:
  6.5 29.7 %all-gather.3.cloned.1.call-start = ((), (), s32[]{:S(2)}) async-start(), calls=%async_computation.1 | async-start | bytes 1179648 | tf_op jit(solution)/shard_map/all_gather | solution.py:8
  7.3 307.9 %all-gather.5.cloned.1.call-start = ((), (), s32[]{:S(2)}) async-start(), calls=%async_computation.2 | async-start | bytes 17825792 | tf_op jit(solution)/shard_map/all_gather | solution.py:9
  300.5 14.7 %copy-start = (f32[64,8,1024]{2,1,0:T(8,128)S(1)}, f32[64,8,1024]{2,1,0:T(8,128)}, u32[]{:S(2)}) copy-start(f32[64,8,1024]{2,1,0:T(8,128)} %param.5) | copy-start | bytes 6291460
Sparse Core Ops, SparseCore 0:
  9.0 27.1 all-gather.2
  38.5 199.9 all-gather.4
where the time goes:
time: 358 us; the launch traced here: 356 us
  blocking collectives  168 us (47%)
  local copies, waits for them, and re-layouts  88 us (25%)
  matrix products  31.7 us (9%)
  waiting for transfers between devices  29.7 us (8%)
  other arithmetic  25.1 us (7%)
  between operations  13.4 us (4%)
    all_to_all x1, blocking collectives, shards(): lax.all_to_all(amplitudes, 'col', split_axis=3, concat_axis=1, tiled=True)  168 us
    unnamed x5, local copies, waits for them, and re-layouts  52.6 us
    all_to_all x3, local copies, waits for them, and re-layouts, shards(): lax.all_to_all(amplitudes, 'col', split_axis=3, concat_axis=1, tiled=True)  32.8 us
    dot_general x1, matrix products, shards(): jnp.einsum('jbia,jbc->aic', lax.all_to_all(amplitudes, 'col', split_axis=...  31.7 us
    all_gather x1, waiting for transfers between devices, shards(): row_weights = lax.all_gather(cycle_weights, 'row', axis=2, tiled=True)  29 us
    all_to_all x1, other arithmetic, shards(): lax.all_to_all(amplitudes, 'col', split_axis=3, concat_axis=1, tiled=True)  25.1 us
  transfers between devices with their start and end apart: 2, of which 1 were waited for; matrix products, arithmetic and copies ran while one was open for 27% of the time, Pallas kernels for 0%

commit v1 on v0

v1 whole, which is shorter than its diff:
```python
import jax
import jax.numpy as jnp
from jax import lax
from jax.experimental import pallas as pl
from jax.experimental.pallas import tpu as pltpu
from jax.sharding import PartitionSpec as P

MESH = pl.DeviceIdType.MESH
F32, BF16 = jnp.float32, jnp.bfloat16


def split(v):
    hi = v.astype(BF16)
    return hi, (v - hi.astype(F32)).astype(BF16)


def kernel(
    amp, wts, out,
    stage, turned, arrived, w_all, w_cross, w_hi, w_lo, l_hi, l_lo, part, relay, final,
    load_sem, wl_sem, w_send, w_recv, core_send, core_recv, z_send, z_recv,
    a_send, a_recv, rel_send, rel_recv, dir_send, dir_recv, mer_send, mer_recv, out_sem,
):
    row, col = lax.axis_index("row"), lax.axis_index("col")
    z, k = row // 2, row % 2
    x, y = col // 4, col % 4
    g = x + k * (y - x)
    s = y + k * (x - y)

    def at(gg, ss):
        return (row, (4 - 3 * k) * (gg % 4) + (1 + 3 * k) * (ss % 4))

    def at_z(zz):
        return (2 * (zz % 4) + k, col)

    other = (2 * z + 1 - k, col)

    def remote(src, dst, send, recv, device):
        return pltpu.make_async_remote_copy(
            src_ref=src, dst_ref=dst, send_sem=send, recv_sem=recv, device_id=device, device_id_type=MESH
        )

    barrier = pltpu.get_barrier_semaphore()
    for d in (1, 2, 3):
        pl.semaphore_signal(barrier, 1, device_id=at(g + d, s), device_id_type=MESH)
        pl.semaphore_signal(barrier, 1, device_id=at(g, s + d), device_id_type=MESH)
    for device in (at_z(z + 1), at_z(z + 3), other):
        pl.semaphore_signal(barrier, 1, device_id=device, device_id_type=MESH)

    half0 = ((s + 2) % 4) // 2

    def block_of(q):
        line0 = 2 * ((g + 1 + q) % 4) + (half0 + q // 4) % 2
        m = q // 2
        u = m // 2
        off = (1 - u) * (2 + m) + u * (3 - m)
        line1 = 2 * ((s + off) % 4) + (g // 2 + 1 + q) % 2
        return line0 + k * (line1 - line0)

    def load(q):
        t = block_of(q)
        return pltpu.make_async_copy(
            amp.at[:, :, :, pl.ds(pl.multiple_of(t * 128, 128), 128)], stage.at[q % 2], load_sem.at[q % 2]
        )

    load(0).start()
    load(1).start()
    own_w = pltpu.make_async_copy(wts, w_all.at[row, g], wl_sem.at[0])
    own_wc = pltpu.make_async_copy(wts, w_cross.at[s], wl_sem.at[1])
    own_w.start()
    own_wc.start()

    pl.semaphore_wait(barrier, 9)

    w_line = [remote(wts, w_all.at[row, g], w_send.at[d], w_recv.at[d], at(g + d + 1, s)) for d in range(3)]
    w_cro = [remote(wts, w_cross.at[s], w_send.at[3 + d], w_recv.at[3 + d], at(g, s + d + 1)) for d in range(3)]
    for copy in w_line + w_cro:
        copy.start()

    def slab(o):
        xx, yy = o // 4, o % 4
        gg = xx + k * (yy - xx)
        r = yy + k * (xx - yy)
        return gg, r

    def send_slab(o):
        gg, r = slab(o)
        return remote(turned.at[o], arrived.at[r, g], a_send.at[o], a_recv.at[4 * r + g], at(gg, s))

    @pl.loop(0, 8)
    def _(q):
        load(q).wait()
        t = block_of(q)
        rows = stage.at[q % 2].reshape(2048, 128)
        for i in range(8):
            v = rows[pl.ds(i, 256, stride=8), :].T
            for e in range(2):
                for h in range(2):
                    turned.at[2 * t + e, h][pl.ds(i, 64, stride=8), :] = v[64 * e : 64 * e + 64, 128 * h : 128 * h + 128]

        @pl.when(q < 6)
        def _():
            load(q + 2).start()

        for e in range(2):
            o = 2 * t + e
            gg, r = slab(o)

            @pl.when(gg != g)
            def _():
                send_slab(o).start()

            @pl.when(gg == g)
            def _():
                pltpu.make_async_copy(turned.at[o], arrived.at[r, g], a_recv.at[4 * r + g]).start()

    def z_copy(n, e, up, sem):
        sl = 2 * (n % 4) + e
        return remote(w_all.at[sl], w_all.at[sl], z_send.at[sem], z_recv.at[sem], at_z(z + 1 if up else z + 3))

    def split_w(n):
        n = n % 4

        @pl.loop(0, 4)
        def _(gg):
            for e in range(2):
                hi, lo = split(w_all[2 * n + e, gg].reshape(256, 128))
                at_rows = pl.ds(pl.multiple_of(gg * 256, 256), 256)
                w_hi[n, at_rows, 128 * e : 128 * e + 128] = hi
                w_lo[n, at_rows, 128 * e : 128 * e + 128] = lo

    own_w.wait()
    own_wc.wait()
    for copy in w_line:
        copy.wait()
    z_copy(z, k, True, k).start()
    z_copy(z, k, False, 2 + k).start()
    for copy in w_cro:
        copy.wait()
    swap = remote(w_cross, w_all.at[row], core_send, core_recv, other)
    swap.start()
    swap.wait()
    z_copy(z, 1 - k, True, 1 - k).start()
    z_copy(z, 1 - k, False, 3 - k).start()
    split_w(z)
    z_copy(z, 0, True, 0).wait()
    z_copy(z + 3, 0, True, 4).start()
    z_copy(z, 1, False, 3).wait()
    z_copy(z + 1, 1, False, 5).start()
    z_copy(z, 1, True, 1).wait()
    z_copy(z, 0, False, 2).wait()
    split_w(z + 3)
    split_w(z + 1)
    z_copy(z + 3, 0, True, 4).wait()
    z_copy(z + 1, 1, False, 5).wait()
    split_w(z + 2)

    def a_arrive(r, gg):
        return remote(turned.at[0], arrived.at[r, gg], a_send.at[0], a_recv.at[4 * r + gg], other)

    def multiply(m, r, then):
        r = r % 4
        for gg in range(4):
            a_arrive(r, gg).wait_recv()

        @pl.loop(0, 4)
        def _(gg):
            for h in range(2):
                hi, lo = split(arrived[r, gg, h])
                lanes = pl.ds(pl.multiple_of(256 * gg + 128 * h, 128), 128)
                l_hi[:, lanes] = hi
                l_lo[:, lanes] = lo

        @pl.loop(0, 4)
        def _(n):
            total = jnp.dot(l_hi[...], w_hi[n], preferred_element_type=F32)
            total += jnp.dot(l_hi[...], w_lo[n], preferred_element_type=F32)
            total += jnp.dot(l_lo[...], w_hi[n], preferred_element_type=F32)
            part[m, n] = total.reshape(64, 8, 256)
            if then is not None:
                then(n)

    low, high = pl.ds(0, 32), pl.ds(32, 32)

    def relay_up(n):
        return remote(part.at[0, n, low], relay.at[0, n], rel_send.at[0, n], rel_recv.at[0, n], at(g, s + 1))

    def relay_down(n):
        return remote(part.at[0, n, high], relay.at[1, n], rel_send.at[1, n], rel_recv.at[1, n], at(g, s + 3))

    def direct_up(n):
        return remote(part.at[1, n, high], final.at[0, n, high], dir_send.at[0, n], dir_recv.at[0, n], at(g, s + 1))

    def direct_down(n):
        return remote(part.at[2, n, low], final.at[1, n, low], dir_send.at[1, n], dir_recv.at[1, n], at(g, s + 3))

    def merged_up(n):
        return remote(part.at[1, n, low], final.at[0, n, low], mer_send.at[0, n], mer_recv.at[0, n], at(g, s + 1))

    def merged_down(n):
        return remote(part.at[2, n, high], final.at[1, n, high], mer_send.at[1, n], mer_recv.at[1, n], at(g, s + 3))

    def send_relays(n):
        relay_up(n).start()
        relay_down(n).start()

    multiply(0, s + 2, send_relays)
    multiply(1, s + 1, lambda n: direct_up(n).start())
    multiply(2, s + 3, lambda n: direct_down(n).start())
    multiply(3, s, None)

    @pl.loop(0, 4)
    def _(n):
        relay_up(n).wait()
        part[1, n, low] += relay[0, n]
        merged_up(n).start()
        relay_down(n).wait()
        part[2, n, high] += relay[1, n]
        merged_down(n).start()

    def put(n):
        return pltpu.make_async_copy(
            part.at[3, n], out.at[:, :, pl.ds(pl.multiple_of(n * 256, 256), 256)], out_sem.at[n]
        )

    @pl.loop(0, 4)
    def _(n):
        direct_up(n).wait()
        direct_down(n).wait()
        merged_up(n).wait()
        merged_down(n).wait()
        part[3, n] += final[0, n] + final[1, n]
        put(n).start()

    for n in range(4):
        put(n).wait()

    @pl.loop(0, 16)
    def _(o):
        gg, r = slab(o)

        @pl.when(gg != g)
        def _():
            send_slab(o).wait_send()


def shards(amplitudes, cycle_weights, residual_in):
    dma = pltpu.SemaphoreType.DMA
    cycle_sum = pl.pallas_call(
        kernel,
        out_shape=jax.ShapeDtypeStruct((64, 8, 1024), F32),
        in_specs=[pl.BlockSpec(memory_space=pl.ANY)] * 2,
        out_specs=pl.BlockSpec(memory_space=pl.ANY),
        scratch_shapes=[
            pltpu.VMEM((2, 4, 64, 8, 128), F32),
            pltpu.VMEM((16, 2, 512, 128), F32),
            pltpu.VMEM((4, 4, 2, 512, 128), F32),
            pltpu.VMEM((8, 4, 4, 64, 128), F32),
            pltpu.VMEM((4, 4, 64, 128), F32),
            pltpu.VMEM((4, 1024, 256), BF16),
            pltpu.VMEM((4, 1024, 256), BF16),
            pltpu.VMEM((512, 1024), BF16),
            pltpu.VMEM((512, 1024), BF16),
            pltpu.VMEM((4, 4, 64, 8, 256), F32),
            pltpu.VMEM((2, 4, 32, 8, 256), F32),
            pltpu.VMEM((2, 4, 64, 8, 256), F32),
            dma((2,)), dma((2,)), dma((6,)), dma((6,)), dma, dma, dma((6,)), dma((6,)),
            dma((16,)), dma((16,)), dma((2, 4)), dma((2, 4)), dma((2, 4)), dma((2, 4)), dma((2, 4)), dma((2, 4)), dma((4,)),
        ],
        compiler_params=pltpu.CompilerParams(collective_id=0, has_side_effects=True, vmem_limit_bytes=60 << 20),
        cost_estimate=pl.CostEstimate(flops=2 * 3 * 512 * 4096 * 1024, bytes_accessed=12 << 20, transcendentals=0),
        name="cycle_sum",
    )(amplitudes, cycle_weights)
    return residual_in + cycle_sum


def solution(mesh):
    return jax.shard_map(
        shards,
        mesh=mesh,
        in_specs=(P(None, "col", "row", None), P(None, "col", "row"), P("col", "row", None)),
        out_specs=P("col", "row", None),
        check_vma=False,
    )
```

time: 358 us -> 102 us (0.28)
  the two profiles are of different devices: /device:TPU:1 before, /device:TPU:8 now
where the time goes in v1:
time: 102 us
  Pallas kernels  98.1 us (96%)
  other arithmetic  3.47 us (3%)
    pallas_call x1, Pallas kernels, shards(): pl.pallas_call(kernel, out_shape=jax.ShapeDtypeStruct((64, 8, 1024), F32)...  98.1 us
    add x1, other arithmetic, shards(): return residual_in + cycle_sum  3.47 us

profile of v1, /device:TPU:8, one launch (start us, length us, event | category | flops | bytes accessed | tf_op | source)
XLA Modules:
  0.0 101.6 jit_solution(1446175284055276468)
XLA Ops:
  0.0 0.0 copy-start
  0.0 98.1 %cycle_sum.1 = f32[64,8,1024]{2,1,0:T(8,128)} custom-call(f32[4,64,8,1024]{3,2,1,0:T(8,128)} %amp.1, f32[4,64,128]{2,1,0:T(8,128)} %wts.1), custom_call_target="tpu_custom_call" | custom-call | flops 12884901888 | bytes 12582912 | tf_op jit(solution)/shard_map/cycle_sum/pallas_call | solution.py:248
  98.2 0.0 copy-done
  98.2 3.5 %add.3 = f32[64,8,1024]{2,1,0:T(8,128)} add(f32[64,8,1024]{2,1,0:T(8,128)S(1)} %copy-done, f32[64,8,1024]{2,1,0:T(8,128)} %cycle_sum.1) | non-fusion elementwise | flops 524288 | bytes 6291456 | tf_op jit(solution)/shard_map/add | solution.py:273
Async XLA Ops:
  0.0 98.2 %copy-start = (f32[64,8,1024]{2,1,0:T(8,128)S(1)}, f32[64,8,1024]{2,1,0:T(8,128)}, u32[]{:S(2)}) copy-start(f32[64,8,1024]{2,1,0:T(8,128)} %param.5) | copy-start | bytes 6291460

commit v2 on v1

--- a/solution.py
+++ b/solution.py
@@ -15,10 +15,10 @@
 
 
 def kernel(
-    amp, wts, out,
+    amp, wts, res, out,
     stage, turned, arrived, w_all, w_cross, w_hi, w_lo, l_hi, l_lo, part, relay, final,
     load_sem, wl_sem, w_send, w_recv, core_send, core_recv, z_send, z_recv,
-    a_send, a_recv, rel_send, rel_recv, dir_send, dir_recv, mer_send, mer_recv, out_sem,
+    a_send, a_recv, rel_send, rel_recv, dir_send, dir_recv, mer_send, mer_recv, res_sem,
 ):
     row, col = lax.axis_index("row"), lax.axis_index("col")
     z, k = row // 2, row % 2
@@ -66,8 +66,11 @@
     load(1).start()
     own_w = pltpu.make_async_copy(wts, w_all.at[row, g], wl_sem.at[0])
     own_wc = pltpu.make_async_copy(wts, w_cross.at[s], wl_sem.at[1])
+    residual = pltpu.make_async_copy(res, out, res_sem)
     own_w.start()
     own_wc.start()
+
+    residual.start()
 
     pl.semaphore_wait(barrier, 9)
 
@@ -217,10 +220,7 @@
         part[2, n, high] += relay[1, n]
         merged_down(n).start()
 
-    def put(n):
-        return pltpu.make_async_copy(
-            part.at[3, n], out.at[:, :, pl.ds(pl.multiple_of(n * 256, 256), 256)], out_sem.at[n]
-        )
+    residual.wait()
 
     @pl.loop(0, 4)
     def _(n):
@@ -228,11 +228,7 @@
         direct_down(n).wait()
         merged_up(n).wait()
         merged_down(n).wait()
-        part[3, n] += final[0, n] + final[1, n]
-        put(n).start()
-
-    for n in range(4):
-        put(n).wait()
+        out[:, :, pl.ds(pl.multiple_of(n * 256, 256), 256)] += part[3, n] + final[0, n] + final[1, n]
 
     @pl.loop(0, 16)
     def _(o):
@@ -245,11 +241,11 @@
 
 def shards(amplitudes, cycle_weights, residual_in):
     dma = pltpu.SemaphoreType.DMA
-    cycle_sum = pl.pallas_call(
+    return pl.pallas_call(
         kernel,
-        out_shape=jax.ShapeDtypeStruct((64, 8, 1024), F32),
-        in_specs=[pl.BlockSpec(memory_space=pl.ANY)] * 2,
-        out_specs=pl.BlockSpec(memory_space=pl.ANY),
+        out_shape=pltpu.VMEM((64, 8, 1024), F32),
+        in_specs=[pl.BlockSpec(memory_space=pl.ANY)] * 3,
+        out_specs=pl.BlockSpec(memory_space=pltpu.VMEM),
         scratch_shapes=[
             pltpu.VMEM((2, 4, 64, 8, 128), F32),
             pltpu.VMEM((16, 2, 512, 128), F32),
@@ -264,13 +260,12 @@
             pltpu.VMEM((2, 4, 32, 8, 256), F32),
             pltpu.VMEM((2, 4, 64, 8, 256), F32),
             dma((2,)), dma((2,)), dma((6,)), dma((6,)), dma, dma, dma((6,)), dma((6,)),
-            dma((16,)), dma((16,)), dma((2, 4)), dma((2, 4)), dma((2, 4)), dma((2, 4)), dma((2, 4)), dma((2, 4)), dma((4,)),
+            dma((16,)), dma((16,)), dma((2, 4)), dma((2, 4)), dma((2, 4)), dma((2, 4)), dma((2, 4)), dma((2, 4)), dma,
         ],
-        compiler_params=pltpu.CompilerParams(collective_id=0, has_side_effects=True, vmem_limit_bytes=60 << 20),
+        compiler_params=pltpu.CompilerParams(collective_id=0, has_side_effects=True, vmem_limit_bytes=54 << 20),
         cost_estimate=pl.CostEstimate(flops=2 * 3 * 512 * 4096 * 1024, bytes_accessed=12 << 20, transcendentals=0),
         name="cycle_sum",
-    )(amplitudes, cycle_weights)
-    return residual_in + cycle_sum
+    )(amplitudes, cycle_weights, residual_in)
 
 
 def solution(mesh):

time: 102 us -> 99 us (0.971)
  other arithmetic: 3.47 us -> 0 us
  local copies, waits for them, and re-layouts: 0.01 us -> 1.32 us
    add x1 -> x0, other arithmetic: 3.47 us -> none  [shards(): return residual_in + cycle_sum]
    unnamed x2 -> x1, local copies, waits for them, and re-layouts: 0.01 us -> 1.32 us
where the time goes in v2:
time: 99 us; the launch traced here: 98.8 us
  Pallas kernels  97.5 us (98%)
  local copies, waits for them, and re-layouts  1.32 us (1%)
    pallas_call x1, Pallas kernels, shards(): pl.pallas_call(kernel, out_shape=pltpu.VMEM((64, 8, 1024), F32), in_specs...  97.5 us

profile of v2, /device:TPU:8, one launch (start us, length us, event | category | flops | bytes accessed | tf_op | source)
XLA Modules:
  0.0 98.8 jit_solution(4432125070190230886)
XLA Ops:
  0.0 97.5 %cycle_sum.1 = f32[64,8,1024]{2,1,0:T(8,128)S(1)} custom-call(f32[4,64,8,1024]{3,2,1,0:T(8,128)} %amp.1, f32[4,64,128]{2,1,0:T(8,128)} %wts.1, f32[64,8,1024]{2,1,0:T(8,128)} %res.1), custom_call_target="tpu_custom_call" | custom-call | flops 12884901888 | bytes 12582912 | tf_op jit(solution)/shard_map/cycle_sum/pallas_call | solution.py:244
  97.5 1.3 %copy.5 = f32[64,8,1024]{2,1,0:T(8,128)} copy(f32[64,8,1024]{2,1,0:T(8,128)S(1)} %cycle_sum.1) | data formatting | bytes 4194304

commit v3 on v2

--- a/solution.py
+++ b/solution.py
@@ -17,7 +17,7 @@
 def kernel(
     amp, wts, res, out,
     stage, turned, arrived, w_all, w_cross, w_hi, w_lo, l_hi, l_lo, part, relay, final,
-    load_sem, wl_sem, w_send, w_recv, core_send, core_recv, z_send, z_recv,
+    load_sem, wl_sem, w_send, w_recv, own_send, own_recv, give_send, give_recv, core_send, core_recv, z_send, z_recv,
     a_send, a_recv, rel_send, rel_recv, dir_send, dir_recv, mer_send, mer_recv, res_sem,
 ):
     row, col = lax.axis_index("row"), lax.axis_index("col")
@@ -42,14 +42,13 @@
     barrier = pltpu.get_barrier_semaphore()
     for d in (1, 2, 3):
         pl.semaphore_signal(barrier, 1, device_id=at(g + d, s), device_id_type=MESH)
-        pl.semaphore_signal(barrier, 1, device_id=at(g, s + d), device_id_type=MESH)
-    for device in (at_z(z + 1), at_z(z + 3), other):
+    for device in (at(g, s + 1), at(g, s + 3), at_z(z + 1), at_z(z + 3), other):
         pl.semaphore_signal(barrier, 1, device_id=device, device_id_type=MESH)
 
     half0 = ((s + 2) % 4) // 2
 
     def block_of(q):
-        line0 = 2 * ((g + 1 + q) % 4) + (half0 + q // 4) % 2
+        line0 = 2 * ((g + 1 + 2 * q + (q // 2) % 2) % 4) + (half0 + q // 4) % 2
         m = q // 2
         u = m // 2
         off = (1 - u) * (2 + m) + u * (3 - m)
@@ -64,20 +63,51 @@
 
     load(0).start()
     load(1).start()
-    own_w = pltpu.make_async_copy(wts, w_all.at[row, g], wl_sem.at[0])
-    own_wc = pltpu.make_async_copy(wts, w_cross.at[s], wl_sem.at[1])
+    own_w = pltpu.make_async_copy(wts, w_all.at[row, 0], wl_sem)
     residual = pltpu.make_async_copy(res, out, res_sem)
     own_w.start()
-    own_wc.start()
 
     residual.start()
 
-    pl.semaphore_wait(barrier, 9)
-
-    w_line = [remote(wts, w_all.at[row, g], w_send.at[d], w_recv.at[d], at(g + d + 1, s)) for d in range(3)]
-    w_cro = [remote(wts, w_cross.at[s], w_send.at[3 + d], w_recv.at[3 + d], at(g, s + d + 1)) for d in range(3)]
-    for copy in w_line + w_cro:
-        copy.start()
+    pl.semaphore_wait(barrier, 8)
+
+    def w_pass(cross, up, onward):
+        step = 1 if up else 3
+        device = at(g, s + step) if cross else at(g + step, s)
+        rows = pl.ds(0 if up else 2, 2)
+        if cross:
+            dst = w_cross.at[1, rows] if onward else w_cross.at[2 if up else 0]
+            src = w_cross.at[2 if up else 0, rows] if onward else wts
+        else:
+            dst = w_all.at[row, 2, rows] if onward else w_all.at[row, 3 if up else 1]
+            src = w_all.at[row, 3 if up else 1, rows] if onward else wts
+        sem = 4 * cross + 2 * onward + (0 if up else 1)
+        return remote(src, dst, w_send.at[sem], w_recv.at[sem], device)
+
+    def own_pass(up, onward):
+        sem = 2 * onward + (0 if up else 1)
+        device = at_z(z + (1 if up else 3))
+        if onward:
+            rows = pl.ds(0 if up else 2, 2)
+            src = w_all.at[2 * ((z + (3 if up else 1)) % 4) + k, 0, rows]
+            return remote(src, src, own_send.at[sem], own_recv.at[sem], device)
+        return remote(wts, w_all.at[row, 0], own_send.at[sem], own_recv.at[sem], device)
+
+    def give(i):
+        if i == 0:
+            src, dst = wts, w_all.at[row, 0]
+        elif i < 3:
+            src = dst = w_all.at[2 * ((z + (3 if i == 1 else 1)) % 4) + k, 0]
+        else:
+            src = dst = w_all.at[2 * ((z + 2) % 4) + k, 0, pl.ds(0 if i == 3 else 2, 2)]
+        return remote(src, dst, give_send.at[i], give_recv.at[i], other)
+
+    for cross in (0, 1):
+        w_pass(cross, True, 0).start()
+        w_pass(cross, False, 0).start()
+    own_pass(True, 0).start()
+    own_pass(False, 0).start()
+    give(0).start()
 
     def slab(o):
         xx, yy = o // 4, o % 4
@@ -87,7 +117,25 @@
 
     def send_slab(o):
         gg, r = slab(o)
-        return remote(turned.at[o], arrived.at[r, g], a_send.at[o], a_recv.at[4 * r + g], at(gg, s))
+        return remote(turned.at[o], arrived.at[r, (g - gg + 4) % 4], a_send.at[o], a_recv.at[4 * r + (g - gg + 4) % 4], at(gg, s))
+
+    def z_copy(n, e, up, sem):
+        sl = 2 * (n % 4) + e
+        rest = w_all.at[sl, pl.ds(1, 3)]
+        return remote(rest, rest, z_send.at[sem], z_recv.at[sem], at_z(z + 1 if up else z + 3))
+
+    def split_w(n):
+        n = n % 4
+
+        @pl.loop(0, 4)
+        def _(gg):
+            for e in range(2):
+                hi, lo = split(w_all[2 * n + e, gg].reshape(256, 128))
+                at_rows = pl.ds(pl.multiple_of(gg * 256, 256), 256)
+                w_hi[n, at_rows, 128 * e : 128 * e + 128] = hi
+                w_lo[n, at_rows, 128 * e : 128 * e + 128] = lo
+
+    swap = remote(w_cross, w_all.at[row, pl.ds(1, 3)], core_send, core_recv, other)
 
     @pl.loop(0, 8)
     def _(q):
@@ -108,57 +156,87 @@
             o = 2 * t + e
             gg, r = slab(o)
 
-            @pl.when(gg != g)
+            @pl.when((gg != g) & (r != s))
             def _():
                 send_slab(o).start()
 
             @pl.when(gg == g)
             def _():
-                pltpu.make_async_copy(turned.at[o], arrived.at[r, g], a_recv.at[4 * r + g]).start()
-
-    def z_copy(n, e, up, sem):
-        sl = 2 * (n % 4) + e
-        return remote(w_all.at[sl], w_all.at[sl], z_send.at[sem], z_recv.at[sem], at_z(z + 1 if up else z + 3))
-
-    def split_w(n):
-        n = n % 4
-
-        @pl.loop(0, 4)
-        def _(gg):
-            for e in range(2):
-                hi, lo = split(w_all[2 * n + e, gg].reshape(256, 128))
-                at_rows = pl.ds(pl.multiple_of(gg * 256, 256), 256)
-                w_hi[n, at_rows, 128 * e : 128 * e + 128] = hi
-                w_lo[n, at_rows, 128 * e : 128 * e + 128] = lo
-
-    own_w.wait()
-    own_wc.wait()
-    for copy in w_line:
-        copy.wait()
-    z_copy(z, k, True, k).start()
-    z_copy(z, k, False, 2 + k).start()
-    for copy in w_cro:
-        copy.wait()
-    swap = remote(w_cross, w_all.at[row], core_send, core_recv, other)
-    swap.start()
-    swap.wait()
-    z_copy(z, 1 - k, True, 1 - k).start()
-    z_copy(z, 1 - k, False, 3 - k).start()
-    split_w(z)
-    z_copy(z, 0, True, 0).wait()
-    z_copy(z + 3, 0, True, 4).start()
-    z_copy(z, 1, False, 3).wait()
-    z_copy(z + 1, 1, False, 5).start()
-    z_copy(z, 1, True, 1).wait()
-    z_copy(z, 0, False, 2).wait()
-    split_w(z + 3)
-    split_w(z + 1)
-    z_copy(z + 3, 0, True, 4).wait()
-    z_copy(z + 1, 1, False, 5).wait()
-    split_w(z + 2)
+                pltpu.make_async_copy(turned.at[o], arrived.at[r, 0], a_recv.at[4 * r]).start()
+
+        @pl.when(q == 1)
+        def _():
+            for cross in (0, 1):
+                w_pass(cross, True, 0).wait()
+                w_pass(cross, True, 1).start()
+                w_pass(cross, False, 0).wait()
+                w_pass(cross, False, 1).start()
+            own_pass(True, 0).wait()
+            own_pass(True, 1).start()
+            give(1).start()
+            own_pass(False, 0).wait()
+            own_pass(False, 1).start()
+            give(2).start()
+
+        @pl.when(q == 3)
+        def _():
+            w_pass(0, True, 1).wait()
+            w_pass(0, False, 1).wait()
+            z_copy(z, k, True, k).start()
+            z_copy(z, k, False, 2 + k).start()
+            w_pass(1, True, 1).wait()
+            w_pass(1, False, 1).wait()
+            swap.start()
+
+        @pl.when(q == 5)
+        def _():
+            swap.wait()
+            z_copy(z, 1 - k, True, 1 - k).start()
+            z_copy(z, 1 - k, False, 3 - k).start()
+            own_pass(True, 1).wait()
+            give(3).start()
+            own_pass(False, 1).wait()
+            give(4).start()
+
+    for d in (1, 3, 2):
+        send_slab(at(g + d, s)[1]).start()
 
     def a_arrive(r, gg):
         return remote(turned.at[0], arrived.at[r, gg], a_send.at[0], a_recv.at[4 * r + gg], other)
+
+    def piece(j):
+        return (z + j + j // 2 - 2 * (j // 3)) % 4
+
+    def weights(j):
+        @pl.when(j == 0)
+        def _():
+            own_w.wait()
+            give(0).wait()
+            split_w(z)
+
+        @pl.when(j == 1)
+        def _():
+            z_copy(z, 0, True, 0).wait()
+            z_copy(z + 3, 0, True, 4).start()
+            z_copy(z, 1, False, 3).wait()
+            z_copy(z + 1, 1, False, 5).start()
+            z_copy(z, 1, True, 1).wait()
+            z_copy(z, 0, False, 2).wait()
+            give(1).wait()
+            give(2).wait()
+            split_w(z + 1)
+
+        @pl.when(j == 2)
+        def _():
+            split_w(z + 3)
+
+        @pl.when(j == 3)
+        def _():
+            z_copy(z + 3, 0, True, 4).wait()
+            z_copy(z + 1, 1, False, 5).wait()
+            give(3).wait()
+            give(4).wait()
+            split_w(z + 2)
 
     def multiply(m, r, then):
         r = r % 4
@@ -174,7 +252,10 @@
                 l_lo[:, lanes] = lo
 
         @pl.loop(0, 4)
-        def _(n):
+        def _(j):
+            n = piece(j)
+            if m == 0:
+                weights(j)
             total = jnp.dot(l_hi[...], w_hi[n], preferred_element_type=F32)
             total += jnp.dot(l_hi[...], w_lo[n], preferred_element_type=F32)
             total += jnp.dot(l_lo[...], w_hi[n], preferred_element_type=F32)
@@ -209,10 +290,10 @@
     multiply(0, s + 2, send_relays)
     multiply(1, s + 1, lambda n: direct_up(n).start())
     multiply(2, s + 3, lambda n: direct_down(n).start())
-    multiply(3, s, None)
 
     @pl.loop(0, 4)
-    def _(n):
+    def _(j):
+        n = piece(j)
         relay_up(n).wait()
         part[1, n, low] += relay[0, n]
         merged_up(n).start()
@@ -220,10 +301,12 @@
         part[2, n, high] += relay[1, n]
         merged_down(n).start()
 
+    multiply(3, s, None)
     residual.wait()
 
     @pl.loop(0, 4)
-    def _(n):
+    def _(j):
+        n = piece(j)
         direct_up(n).wait()
         direct_down(n).wait()
         merged_up(n).wait()
@@ -251,7 +334,7 @@
             pltpu.VMEM((16, 2, 512, 128), F32),
             pltpu.VMEM((4, 4, 2, 512, 128), F32),
             pltpu.VMEM((8, 4, 4, 64, 128), F32),
-            pltpu.VMEM((4, 4, 64, 128), F32),
+            pltpu.VMEM((3, 4, 64, 128), F32),
             pltpu.VMEM((4, 1024, 256), BF16),
             pltpu.VMEM((4, 1024, 256), BF16),
             pltpu.VMEM((512, 1024), BF16),
@@ -259,7 +342,7 @@
             pltpu.VMEM((4, 4, 64, 8, 256), F32),
             pltpu.VMEM((2, 4, 32, 8, 256), F32),
             pltpu.VMEM((2, 4, 64, 8, 256), F32),
-            dma((2,)), dma((2,)), dma((6,)), dma((6,)), dma, dma, dma((6,)), dma((6,)),
+            dma((2,)), dma, dma((8,)), dma((8,)), dma((4,)), dma((4,)), dma((5,)), dma((5,)), dma, dma, dma((6,)), dma((6,)),
             dma((16,)), dma((16,)), dma((2, 4)), dma((2, 4)), dma((2, 4)), dma((2, 4)), dma((2, 4)), dma((2, 4)), dma,
         ],
         compiler_params=pltpu.CompilerParams(collective_id=0, has_side_effects=True, vmem_limit_bytes=54 << 20),

time: 99 us -> 94.6 us (0.956)
  the two profiles are of different devices: /device:TPU:8 before, /device:TPU:1 now
where the time goes in v3:
time: 94.6 us; the launch traced here: 94.5 us
  Pallas kernels  93.2 us (99%)
  local copies, waits for them, and re-layouts  1.32 us (1%)
    pallas_call x1, Pallas kernels, shards(): pl.pallas_call(kernel, out_shape=pltpu.VMEM((64, 8, 1024), F32), in_specs...  93.2 us

profile of v3, /device:TPU:1, one launch (start us, length us, event | category | flops | bytes accessed | tf_op | source)
XLA Modules:
  0.0 94.5 jit_solution(16271178616989692702)
XLA Ops:
  0.0 93.2 %cycle_sum.1 = f32[64,8,1024]{2,1,0:T(8,128)S(1)} custom-call(f32[4,64,8,1024]{3,2,1,0:T(8,128)} %amp.1, f32[4,64,128]{2,1,0:T(8,128)} %wts.1, f32[64,8,1024]{2,1,0:T(8,128)} %res.1), custom_call_target="tpu_custom_call" | custom-call | flops 12884901888 | bytes 12582912 | tf_op jit(solution)/shard_map/cycle_sum/pallas_call | solution.py:327
  93.2 1.3 %copy.5 = f32[64,8,1024]{2,1,0:T(8,128)} copy(f32[64,8,1024]{2,1,0:T(8,128)S(1)} %cycle_sum.1) | data formatting | bytes 4194304

commit v4 on v3

--- a/solution.py
+++ b/solution.py
@@ -17,8 +17,8 @@
 def kernel(
     amp, wts, res, out,
     stage, turned, arrived, w_all, w_cross, w_hi, w_lo, l_hi, l_lo, part, relay, final,
-    load_sem, wl_sem, w_send, w_recv, own_send, own_recv, give_send, give_recv, core_send, core_recv, z_send, z_recv,
-    a_send, a_recv, rel_send, rel_recv, dir_send, dir_recv, mer_send, mer_recv, res_sem,
+    load_sem, wl_sem, res_sem, w_send, z_send, a_send, p_send,
+    w_recv, own_recv, give_recv, core_recv, z_recv, a_recv, rel_recv, dir_recv, mer_recv,
 ):
     row, col = lax.axis_index("row"), lax.axis_index("col")
     z, k = row // 2, row % 2
@@ -38,6 +38,9 @@
         return pltpu.make_async_remote_copy(
             src_ref=src, dst_ref=dst, send_sem=send, recv_sem=recv, device_id=device, device_id_type=MESH
         )
+
+    def take(ref, sem):
+        pltpu.make_async_copy(ref, ref, sem).wait()
 
     barrier = pltpu.get_barrier_semaphore()
     for d in (1, 2, 3):
@@ -81,17 +84,15 @@
         else:
             dst = w_all.at[row, 2, rows] if onward else w_all.at[row, 3 if up else 1]
             src = w_all.at[row, 3 if up else 1, rows] if onward else wts
-        sem = 4 * cross + 2 * onward + (0 if up else 1)
-        return remote(src, dst, w_send.at[sem], w_recv.at[sem], device)
+        return remote(src, dst, w_send, w_recv.at[1 + cross if onward else 0], device)
 
     def own_pass(up, onward):
-        sem = 2 * onward + (0 if up else 1)
         device = at_z(z + (1 if up else 3))
         if onward:
             rows = pl.ds(0 if up else 2, 2)
             src = w_all.at[2 * ((z + (3 if up else 1)) % 4) + k, 0, rows]
-            return remote(src, src, own_send.at[sem], own_recv.at[sem], device)
-        return remote(wts, w_all.at[row, 0], own_send.at[sem], own_recv.at[sem], device)
+            return remote(src, src, w_send, own_recv.at[1], device)
+        return remote(wts, w_all.at[row, 0], w_send, own_recv.at[0], device)
 
     def give(i):
         if i == 0:
@@ -100,7 +101,7 @@
             src = dst = w_all.at[2 * ((z + (3 if i == 1 else 1)) % 4) + k, 0]
         else:
             src = dst = w_all.at[2 * ((z + 2) % 4) + k, 0, pl.ds(0 if i == 3 else 2, 2)]
-        return remote(src, dst, give_send.at[i], give_recv.at[i], other)
+        return remote(src, dst, w_send, give_recv.at[(i + 1) // 2], other)
 
     for cross in (0, 1):
         w_pass(cross, True, 0).start()
@@ -117,12 +118,12 @@
 
     def send_slab(o):
         gg, r = slab(o)
-        return remote(turned.at[o], arrived.at[r, (g - gg + 4) % 4], a_send.at[o], a_recv.at[4 * r + (g - gg + 4) % 4], at(gg, s))
-
-    def z_copy(n, e, up, sem):
+        return remote(turned.at[o], arrived.at[r, (g - gg + 4) % 4], a_send, a_recv.at[r], at(gg, s))
+
+    def z_copy(n, e, up, onward):
         sl = 2 * (n % 4) + e
         rest = w_all.at[sl, pl.ds(1, 3)]
-        return remote(rest, rest, z_send.at[sem], z_recv.at[sem], at_z(z + 1 if up else z + 3))
+        return remote(rest, rest, z_send, z_recv.at[2 if onward else (e if up else 1 - e)], at_z(z + 1 if up else z + 3))
 
     def split_w(n):
         n = n % 4
@@ -135,7 +136,7 @@
                 w_hi[n, at_rows, 128 * e : 128 * e + 128] = hi
                 w_lo[n, at_rows, 128 * e : 128 * e + 128] = lo
 
-    swap = remote(w_cross, w_all.at[row, pl.ds(1, 3)], core_send, core_recv, other)
+    swap = remote(w_cross, w_all.at[row, pl.ds(1, 3)], w_send, core_recv, other)
 
     @pl.loop(0, 8)
     def _(q):
@@ -162,48 +163,40 @@
 
             @pl.when(gg == g)
             def _():
-                pltpu.make_async_copy(turned.at[o], arrived.at[r, 0], a_recv.at[4 * r]).start()
+                pltpu.make_async_copy(turned.at[o], arrived.at[r, 0], a_recv.at[r]).start()
 
         @pl.when(q == 1)
         def _():
+            take(w_all.at[0], w_recv.at[0])
             for cross in (0, 1):
-                w_pass(cross, True, 0).wait()
                 w_pass(cross, True, 1).start()
-                w_pass(cross, False, 0).wait()
                 w_pass(cross, False, 1).start()
-            own_pass(True, 0).wait()
+            take(w_all.at[0, pl.ds(0, 2)], own_recv.at[0])
             own_pass(True, 1).start()
+            own_pass(False, 1).start()
             give(1).start()
-            own_pass(False, 0).wait()
-            own_pass(False, 1).start()
             give(2).start()
 
         @pl.when(q == 3)
         def _():
-            w_pass(0, True, 1).wait()
-            w_pass(0, False, 1).wait()
-            z_copy(z, k, True, k).start()
-            z_copy(z, k, False, 2 + k).start()
-            w_pass(1, True, 1).wait()
-            w_pass(1, False, 1).wait()
+            take(w_all.at[0, 0], w_recv.at[1])
+            z_copy(z, k, True, 0).start()
+            z_copy(z, k, False, 0).start()
+            take(w_all.at[0, 0], w_recv.at[2])
             swap.start()
 
         @pl.when(q == 5)
         def _():
-            swap.wait()
-            z_copy(z, 1 - k, True, 1 - k).start()
-            z_copy(z, 1 - k, False, 3 - k).start()
-            own_pass(True, 1).wait()
+            take(w_cross, core_recv)
+            z_copy(z, 1 - k, True, 0).start()
+            z_copy(z, 1 - k, False, 0).start()
+            take(w_all.at[0, 0], own_recv.at[1])
             give(3).start()
-            own_pass(False, 1).wait()
             give(4).start()
 
     for d in (1, 3, 2):
         send_slab(at(g + d, s)[1]).start()
 
-    def a_arrive(r, gg):
-        return remote(turned.at[0], arrived.at[r, gg], a_send.at[0], a_recv.at[4 * r + gg], other)
-
     def piece(j):
         return (z + j + j // 2 - 2 * (j // 3)) % 4
 
@@ -211,19 +204,16 @@
         @pl.when(j == 0)
         def _():
             own_w.wait()
-            give(0).wait()
+            take(w_all.at[0, 0], give_recv.at[0])
             split_w(z)
 
         @pl.when(j == 1)
         def _():
-            z_copy(z, 0, True, 0).wait()
-            z_copy(z + 3, 0, True, 4).start()
-            z_copy(z, 1, False, 3).wait()
-            z_copy(z + 1, 1, False, 5).start()
-            z_copy(z, 1, True, 1).wait()
-            z_copy(z, 0, False, 2).wait()
-            give(1).wait()
-            give(2).wait()
+            take(w_all.at[pl.ds(0, 2), pl.ds(1, 3)], z_recv.at[0])
+            z_copy(z + 3, 0, True, 1).start()
+            z_copy(z + 1, 1, False, 1).start()
+            take(w_all.at[pl.ds(0, 2), pl.ds(1, 3)], z_recv.at[1])
+            take(w_all.at[0, pl.ds(0, 2)], give_recv.at[1])
             split_w(z + 1)
 
         @pl.when(j == 2)
@@ -232,16 +222,13 @@
 
         @pl.when(j == 3)
         def _():
-            z_copy(z + 3, 0, True, 4).wait()
-            z_copy(z + 1, 1, False, 5).wait()
-            give(3).wait()
-            give(4).wait()
+            take(w_all.at[pl.ds(0, 2), pl.ds(1, 3)], z_recv.at[2])
+            take(w_all.at[0, 0], give_recv.at[2])
             split_w(z + 2)
 
     def multiply(m, r, then):
         r = r % 4
-        for gg in range(4):
-            a_arrive(r, gg).wait_recv()
+        take(arrived.at[r], a_recv.at[r])
 
         @pl.loop(0, 4)
         def _(gg):
@@ -266,22 +253,22 @@
     low, high = pl.ds(0, 32), pl.ds(32, 32)
 
     def relay_up(n):
-        return remote(part.at[0, n, low], relay.at[0, n], rel_send.at[0, n], rel_recv.at[0, n], at(g, s + 1))
+        return remote(part.at[0, n, low], relay.at[0, n], p_send, rel_recv.at[n], at(g, s + 1))
 
     def relay_down(n):
-        return remote(part.at[0, n, high], relay.at[1, n], rel_send.at[1, n], rel_recv.at[1, n], at(g, s + 3))
+        return remote(part.at[0, n, high], relay.at[1, n], p_send, rel_recv.at[n], at(g, s + 3))
 
     def direct_up(n):
-        return remote(part.at[1, n, high], final.at[0, n, high], dir_send.at[0, n], dir_recv.at[0, n], at(g, s + 1))
+        return remote(part.at[1, n, high], final.at[0, n, high], p_send, dir_recv, at(g, s + 1))
 
     def direct_down(n):
-        return remote(part.at[2, n, low], final.at[1, n, low], dir_send.at[1, n], dir_recv.at[1, n], at(g, s + 3))
+        return remote(part.at[2, n, low], final.at[1, n, low], p_send, dir_recv, at(g, s + 3))
 
     def merged_up(n):
-        return remote(part.at[1, n, low], final.at[0, n, low], mer_send.at[0, n], mer_recv.at[0, n], at(g, s + 1))
+        return remote(part.at[1, n, low], final.at[0, n, low], p_send, mer_recv.at[n], at(g, s + 1))
 
     def merged_down(n):
-        return remote(part.at[2, n, high], final.at[1, n, high], mer_send.at[1, n], mer_recv.at[1, n], at(g, s + 3))
+        return remote(part.at[2, n, high], final.at[1, n, high], p_send, mer_recv.at[n], at(g, s + 3))
 
     def send_relays(n):
         relay_up(n).start()
@@ -294,32 +281,26 @@
     @pl.loop(0, 4)
     def _(j):
         n = piece(j)
-        relay_up(n).wait()
+        take(relay.at[:, n], rel_recv.at[n])
         part[1, n, low] += relay[0, n]
         merged_up(n).start()
-        relay_down(n).wait()
         part[2, n, high] += relay[1, n]
         merged_down(n).start()
 
     multiply(3, s, None)
     residual.wait()
+    take(final.at[0], dir_recv)
 
     @pl.loop(0, 4)
     def _(j):
         n = piece(j)
-        direct_up(n).wait()
-        direct_down(n).wait()
-        merged_up(n).wait()
-        merged_down(n).wait()
+        take(final.at[0, n], mer_recv.at[n])
         out[:, :, pl.ds(pl.multiple_of(n * 256, 256), 256)] += part[3, n] + final[0, n] + final[1, n]
 
-    @pl.loop(0, 16)
-    def _(o):
-        gg, r = slab(o)
-
-        @pl.when(gg != g)
-        def _():
-            send_slab(o).wait_send()
+    take(w_all.at[pl.ds(0, 4)], w_send)
+    take(w_all.at[pl.ds(0, 6), pl.ds(1, 3)], z_send)
+    take(turned.at[pl.ds(0, 12)], a_send)
+    take(part.at[pl.ds(0, 3)], p_send)
 
 
 def shards(amplitudes, cycle_weights, residual_in):
@@ -342,8 +323,8 @@
             pltpu.VMEM((4, 4, 64, 8, 256), F32),
             pltpu.VMEM((2, 4, 32, 8, 256), F32),
             pltpu.VMEM((2, 4, 64, 8, 256), F32),
-            dma((2,)), dma, dma((8,)), dma((8,)), dma((4,)), dma((4,)), dma((5,)), dma((5,)), dma, dma, dma((6,)), dma((6,)),
-            dma((16,)), dma((16,)), dma((2, 4)), dma((2, 4)), dma((2, 4)), dma((2, 4)), dma((2, 4)), dma((2, 4)), dma,
+            dma((2,)), dma, dma, dma, dma, dma, dma,
+            dma((3,)), dma((2,)), dma((3,)), dma, dma((3,)), dma((4,)), dma((4,)), dma, dma((4,)),
         ],
         compiler_params=pltpu.CompilerParams(collective_id=0, has_side_effects=True, vmem_limit_bytes=54 << 20),
         cost_estimate=pl.CostEstimate(flops=2 * 3 * 512 * 4096 * 1024, bytes_accessed=12 << 20, transcendentals=0),

time: 94.6 us -> 93.5 us (0.988)
  Pallas kernels: 93.2 us -> 92 us
    pallas_call x1, Pallas kernels: 93.2 us -> 92 us  [shards(): pl.pallas_call(kernel, out_shape=pltpu.VMEM((64, 8, 1024), F32), in_specs...]
where the time goes in v4:
time: 93.5 us; the launch traced here: 93.4 us
  Pallas kernels  92 us (98%)
  local copies, waits for them, and re-layouts  1.32 us (1%)
    pallas_call x1, Pallas kernels, shards(): pl.pallas_call(kernel, out_shape=pltpu.VMEM((64, 8, 1024), F32), in_specs...  92 us

profile of v4, /device:TPU:1, one launch (start us, length us, event | category | flops | bytes accessed | tf_op | source)
XLA Modules:
  0.0 93.4 jit_solution(472741397252446565)
XLA Ops:
  0.0 92.0 %cycle_sum.1 = f32[64,8,1024]{2,1,0:T(8,128)S(1)} custom-call(f32[4,64,8,1024]{3,2,1,0:T(8,128)} %amp.1, f32[4,64,128]{2,1,0:T(8,128)} %wts.1, f32[64,8,1024]{2,1,0:T(8,128)} %res.1), custom_call_target="tpu_custom_call" | custom-call | flops 12884901888 | bytes 12582912 | tf_op jit(solution)/shard_map/cycle_sum/pallas_call | solution.py:308
  92.0 1.3 %copy.5 = f32[64,8,1024]{2,1,0:T(8,128)} copy(f32[64,8,1024]{2,1,0:T(8,128)S(1)} %cycle_sum.1) | data formatting | bytes 4194304

commit v5 on v4

--- a/solution.py
+++ b/solution.py
@@ -55,7 +55,7 @@
         m = q // 2
         u = m // 2
         off = (1 - u) * (2 + m) + u * (3 - m)
-        line1 = 2 * ((s + off) % 4) + (g // 2 + 1 + q) % 2
+        line1 = 2 * ((s + off) % 4) + (g // 2 + q) % 2
         return line0 + k * (line1 - line0)
 
     def load(q):
@@ -291,11 +291,20 @@
     residual.wait()
     take(final.at[0], dir_recv)
 
+    def lanes(n):
+        return pl.ds(pl.multiple_of(n * 256, 256), 256)
+
+    @pl.loop(0, 4)
+    def _(n):
+        out[:32, :, lanes(n)] += part[3, n, low] + final[1, n, low]
+        out[32:, :, lanes(n)] += part[3, n, high] + final[0, n, high]
+
     @pl.loop(0, 4)
     def _(j):
         n = piece(j)
         take(final.at[0, n], mer_recv.at[n])
-        out[:, :, pl.ds(pl.multiple_of(n * 256, 256), 256)] += part[3, n] + final[0, n] + final[1, n]
+        out[:32, :, lanes(n)] += final[0, n, low]
+        out[32:, :, lanes(n)] += final[1, n, high]
 
     take(w_all.at[pl.ds(0, 4)], w_send)
     take(w_all.at[pl.ds(0, 6), pl.ds(1, 3)], z_send)

time: 93.5 us -> 93.5 us (level)
  no operation moved by 1% of the time
where the time goes in v5:
time: 93.5 us; the launch traced here: 93.3 us
  Pallas kernels  92 us (98%)
  local copies, waits for them, and re-layouts  1.32 us (1%)
    pallas_call x1, Pallas kernels, shards(): pl.pallas_call(kernel, out_shape=pltpu.VMEM((64, 8, 1024), F32), in_specs...  92 us

profile of v5, /device:TPU:1, one launch (start us, length us, event | category | flops | bytes accessed | tf_op | source)
XLA Modules:
  0.0 93.3 jit_solution(5553704215655143286)
XLA Ops:
  0.0 92.0 %cycle_sum.1 = f32[64,8,1024]{2,1,0:T(8,128)S(1)} custom-call(f32[4,64,8,1024]{3,2,1,0:T(8,128)} %amp.1, f32[4,64,128]{2,1,0:T(8,128)} %wts.1, f32[64,8,1024]{2,1,0:T(8,128)} %res.1), custom_call_target="tpu_custom_call" | custom-call | flops 12884901888 | bytes 12582912 | tf_op jit(solution)/shard_map/cycle_sum/pallas_call | solution.py:317
  92.0 1.3 %copy.5 = f32[64,8,1024]{2,1,0:T(8,128)} copy(f32[64,8,1024]{2,1,0:T(8,128)S(1)} %cycle_sum.1) | data formatting | bytes 4194304

commit v6 on v5

--- a/solution.py
+++ b/solution.py
@@ -253,10 +253,10 @@
     low, high = pl.ds(0, 32), pl.ds(32, 32)
 
     def relay_up(n):
-        return remote(part.at[0, n, low], relay.at[0, n], p_send, rel_recv.at[n], at(g, s + 1))
+        return remote(part.at[0, n, low], relay.at[0, n], p_send, rel_recv.at[0, n], at(g, s + 1))
 
     def relay_down(n):
-        return remote(part.at[0, n, high], relay.at[1, n], p_send, rel_recv.at[n], at(g, s + 3))
+        return remote(part.at[0, n, high], relay.at[1, n], p_send, rel_recv.at[1, n], at(g, s + 3))
 
     def direct_up(n):
         return remote(part.at[1, n, high], final.at[0, n, high], p_send, dir_recv, at(g, s + 1))
@@ -281,9 +281,10 @@
     @pl.loop(0, 4)
     def _(j):
         n = piece(j)
-        take(relay.at[:, n], rel_recv.at[n])
+        take(relay.at[0, n], rel_recv.at[0, n])
         part[1, n, low] += relay[0, n]
         merged_up(n).start()
+        take(relay.at[1, n], rel_recv.at[1, n])
         part[2, n, high] += relay[1, n]
         merged_down(n).start()
 
@@ -333,7 +334,7 @@
             pltpu.VMEM((2, 4, 32, 8, 256), F32),
             pltpu.VMEM((2, 4, 64, 8, 256), F32),
             dma((2,)), dma, dma, dma, dma, dma, dma,
-            dma((3,)), dma((2,)), dma((3,)), dma, dma((3,)), dma((4,)), dma((4,)), dma, dma((4,)),
+            dma((3,)), dma((2,)), dma((3,)), dma, dma((3,)), dma((4,)), dma((2, 4)), dma, dma((4,)),
         ],
         compiler_params=pltpu.CompilerParams(collective_id=0, has_side_effects=True, vmem_limit_bytes=54 << 20),
         cost_estimate=pl.CostEstimate(flops=2 * 3 * 512 * 4096 * 1024, bytes_accessed=12 << 20, transcendentals=0),

time: 93.5 us -> 93.5 us (level)
  no operation moved by 1% of the time
where the time goes in v6:
time: 93.5 us; the launch traced here: 93.4 us
  Pallas kernels  92 us (98%)
  local copies, waits for them, and re-layouts  1.32 us (1%)
    pallas_call x1, Pallas kernels, shards(): pl.pallas_call(kernel, out_shape=pltpu.VMEM((64, 8, 1024), F32), in_specs...  92 us

profile of v6, /device:TPU:1, one launch (start us, length us, event | category | flops | bytes accessed | tf_op | source)
XLA Modules:
  0.0 93.4 jit_solution(13586375262039600201)
XLA Ops:
  0.0 92.0 %cycle_sum.1 = f32[64,8,1024]{2,1,0:T(8,128)S(1)} custom-call(f32[4,64,8,1024]{3,2,1,0:T(8,128)} %amp.1, f32[4,64,128]{2,1,0:T(8,128)} %wts.1, f32[64,8,1024]{2,1,0:T(8,128)} %res.1), custom_call_target="tpu_custom_call" | custom-call | flops 12884901888 | bytes 12582912 | tf_op jit(solution)/shard_map/cycle_sum/pallas_call | solution.py:318
  92.1 1.3 %copy.5 = f32[64,8,1024]{2,1,0:T(8,128)} copy(f32[64,8,1024]{2,1,0:T(8,128)S(1)} %cycle_sum.1) | data formatting | bytes 4194304
